TPU v7x, 512 devices: a whole 4x4x16 slice. The times are simulated.
512 devices in a mesh: nodes: 128 (over x, z, core), feat: 4 (over y).
Axes of the slice: x: 4, y: 4, z: 16, core: 2. Of those that a mesh axis runs over, the one named last changes fastest.
Arguments:
- x_batch: bfloat16 [49152, 256], P('nodes', 'feat'), may hold values from -6 to 6
- tiles: bfloat16 [128, 128, 2, 128, 128], P('nodes', None, None, 'feat'), may hold values from -0.0546875 to 0.0546875
- tile_src: int32 [128, 128, 2], P('nodes'), may hold values from 0 to 2
- tile_dst: int32 [128, 128, 2], P(None, 'nodes'), may hold values from 0 to 2
- history: bfloat16 [262144, 256], P('nodes', 'feat'), may hold values from -6 to 6
- halo_ids: int32 [384, 128], P('nodes'), may hold values from 0 to 262143, as said below
- halo_adj: bfloat16 [384, 128, 128], P('nodes'), may hold values from -0.5 to 0.5
- weight: bfloat16 [256, 256], P('feat'), may hold values from -0.375 to 0.375
Outputs:
- new_embed: bfloat16 [49152, 256], P('nodes', 'feat')
Inputs may be any that keep to these rules, and one draw needn't show every extreme that they name: `halo_ids`: node i lies on device i // 2048 of nodes. Among the 384 ids of one device's clusters at most 9 lie on any one device, and for every device some one device holds exactly 9 of them.
All inputs are finite; a program needn't handle non-finite values.
Results may differ from a plain program's by a relative error of at most 0.0051.
Values may be sent and summed in bfloat16 or wider, within the bound.
A program may use at most 128 MiB of HBM per device.

v0:
```python
import jax
import jax.numpy as jnp
from jax import lax
from jax.sharding import PartitionSpec as P


def per_device(x_batch, tiles, tile_src, tile_dst, history, halo_ids, halo_adj, weight):
    peer_count = lax.axis_size("nodes")
    clusters = halo_adj.shape[0]
    cluster_size = halo_adj.shape[1]
    feat_cols = x_batch.shape[1]
    src_code = tile_src.astype(jnp.bfloat16)
    got_tiles, got_code = (
        lax.all_to_all(tiles, "nodes", split_axis=1, concat_axis=0, tiled=True),
        lax.all_to_all(src_code, "nodes", split_axis=1, concat_axis=0, tiled=True),
    )
    all_x = lax.all_gather(x_batch, "nodes", axis=0, tiled=True).reshape(
        -1, cluster_size, feat_cols
    )
    holder_base = jnp.arange(peer_count, dtype=jnp.int32)[:, None, None] * clusters
    source_ids = holder_base + got_code.astype(jnp.int32)
    got_x = all_x[source_ids]
    full_tiles = lax.all_gather(got_tiles, "feat", axis=3, tiled=True)
    blocks = full_tiles.reshape(-1, cluster_size, cluster_size)
    block_x = got_x.reshape(-1, cluster_size, feat_cols)
    products = jnp.einsum("tij,tjf->tif", blocks, block_x, preferred_element_type=jnp.float32)
    dst_onehot = (tile_dst.reshape(-1)[:, None] == jnp.arange(clusters, dtype=jnp.int32)).astype(
        jnp.float32
    )
    tile_sum = jnp.einsum("tc,tif->cif", dst_onehot, products, precision=lax.Precision.HIGHEST)
    halo_flat = halo_ids.reshape(-1)
    node_rows = history.shape[0]
    halo_total = halo_flat.shape[0]
    slot_cap = 3 * halo_total // peer_count
    owners = halo_flat // node_rows
    local_rows = halo_flat - owners * node_rows
    owner_hits = (owners[:, None] == jnp.arange(peer_count, dtype=jnp.int32)[None, :]).astype(
        jnp.int32
    )
    slot_rank = jnp.sum(jnp.cumsum(owner_hits, 0) * owner_hits, 1) - 1
    slot_index = owners * slot_cap + slot_rank
    requests = jnp.zeros((peer_count * slot_cap,), jnp.int32).at[slot_index].set(local_rows)
    requests = requests.reshape(peer_count, slot_cap)
    served = history[lax.all_to_all(requests, "nodes", split_axis=0, concat_axis=0, tiled=True)]
    fetched = lax.all_to_all(served, "nodes", split_axis=0, concat_axis=0, tiled=True)
    halo_x = fetched.reshape(peer_count * slot_cap, feat_cols)[slot_index].reshape(
        clusters, -1, feat_cols
    )
    halo_term = jnp.einsum("crh,chf->crf", halo_adj, halo_x, preferred_element_type=jnp.float32)
    aggregate = (
        (tile_sum + halo_term).astype(jnp.bfloat16).reshape(clusters * cluster_size, feat_cols)
    )
    partial_act = jnp.dot(aggregate, weight, preferred_element_type=jnp.float32)
    pre_act = lax.psum_scatter(partial_act, "feat", scatter_dimension=1, tiled=True)
    return jax.nn.silu(pre_act).astype(jnp.bfloat16)


def solution(mesh):
    return jax.shard_map(
        per_device,
        mesh=mesh,
        in_specs=(
            P("nodes", "feat"),
            P("nodes", None, None, "feat", None),
            P("nodes", None, None),
            P(None, "nodes", None),
            P("nodes", "feat"),
            P("nodes", None),
            P("nodes", None, None),
            P("feat", None),
        ),
        out_specs=P("nodes", "feat"),
        check_vma=False,
    )
```

profile of v0, /device:TPU:2, one launch (start us, length us, event | category | flops | bytes accessed | tf_op | source)
XLA Modules:
  0.0 338.5 jit_solution(13165212099762185309)
XLA Ops:
  6.6 0.7 all-gather.4.cloned.1.call-update
  7.3 122.9 %all_to_all.38 = bf16[1,128,2,32,128]{4,3,2,0,1:T(8,128)(2,1)} all-to-all(bf16[1,128,2,32,128]{4,3,2,0,1:T(8,128)(2,1)} %bitcast.79), channel_id=1, replica_groups=mesh['nodes'=128,'feat'=4] {'nodes'}, dimensions={1} | all-to-all | bytes 4194304 | tf_op jit(solution)/shard_map/all_to_all | solution.py:14
  130.4 0.2 fusion.8
  130.7 0.2 fusion.10
  131.0 2.9 scatter_custom_fusion
  133.9 0.8 all_to_all.30
  134.8 8.5 %all-to-all-start.2 = ((s32[128,1,9]{2,1,0:T(1,128)}), s32[128,1,9]{2,1,0:T(1,128)S(1)}, u32[]{:S(2)}, u32[]{:S(2)}) async-start(s32[128,1,9]{2,1,0:T(1,128)} %bitcast.9), calls=%async_computation.2 | async-start | bytes 131072 | tf_op jit(solution)/shard_map/all_to_all | solution.py:44
  143.3 0.8 copy.30
  144.1 0.3 copy.37
  144.4 13.8 %all-to-all-done.2 = s32[128,1,9]{2,1,0:T(1,128)S(1)} async-done(((s32[128,1,9]{2,1,0:T(1,128)}), s32[128,1,9]{2,1,0:T(1,128)S(1)}, u32[]{:S(2)}, u32[]{:S(2)}) %all-to-all-start.2) | async-done | bytes 4640 | tf_op jit(solution)/shard_map/all_to_all | solution.py:44
  158.2 7.3 %all-to-all-start = ((bf16[1,128,2]{2,0,1:T(2,128)(2,1)}), bf16[1,128,2]{2,0,1:T(2,128)(2,1)S(1)}, u32[]{:S(2)}, u32[]{:S(2)}) async-start(bf16[1,128,2]{2,0,1:T(2,128)(2,1)} %copy.30), calls=%async_computation | async-start | bytes 131072 | tf_op jit(solution)/shard_map/all_to_all | solution.py:15
  165.5 0.2 reshape.262
  165.7 2.9 gather_fusion.1
  168.6 0.1 reshape.261
  168.8 1.1 reshape.294
  169.9 10.7 %all-to-all-done = bf16[1,128,2]{2,0,1:T(2,128)(2,1)S(1)} async-done(((bf16[1,128,2]{2,0,1:T(2,128)(2,1)}), bf16[1,128,2]{2,0,1:T(2,128)(2,1)S(1)}, u32[]{:S(2)}, u32[]{:S(2)}) %all-to-all-start) | async-done | bytes 544 | tf_op jit(solution)/shard_map/all_to_all | solution.py:15
  180.6 7.3 %all-to-all-start.3 = ((bf16[128,2,288]{2,1,0:T(2,128)(2,1)}), bf16[128,2,288]{2,1,0:T(2,128)(2,1)S(1)}, u32[]{:S(2)}, u32[]{:S(2)}) async-start(bf16[128,2,288]{2,1,0:T(2,128)(2,1)} %reshape.294), calls=%async_computation.3 | async-start | bytes 393216 | tf_op jit(solution)/shard_map/all_to_all | solution.py:45
  188.0 0.1 eq.36
  188.4 0.1 reshape.254
  188.5 19.2 %all-to-all-done.3 = bf16[128,2,288]{2,1,0:T(2,128)(2,1)S(1)} async-done(((bf16[128,2,288]{2,1,0:T(2,128)(2,1)}), bf16[128,2,288]{2,1,0:T(2,128)(2,1)S(1)}, u32[]{:S(2)}, u32[]{:S(2)}) %all-to-all-start.3) | async-done | bytes 147488 | tf_op jit(solution)/shard_map/all_to_all | solution.py:45
  207.8 0.4 reshape.295
  208.2 0.2 reshape.248
  208.3 1.6 gather_fusion.2
  210.0 0.2 fusion.26
  210.2 7.7 %copy_bitcast_fusion = bf16[384,128,64]{1,2,0:T(8,128)(2,1)} fusion(bf16[49152,64]{0,1:T(8,128)(2,1)} %all-gather.4.cloned.1.call-done), kind=kLoop, calls=%fused_computation.6 | loop fusion | bytes 12582912 | tf_op jit(solution)/shard_map/reshape | solution.py:17
  217.9 5.8 %gather_fusion = bf16[256,128,64]{1,2,0:T(8,128)(2,1)} fusion(bf16[384,128,64]{1,2,0:T(8,128)(2,1)} %copy_bitcast_fusion, s32[1024]{0:T(1024)S(1)} %pad_clamp_fusion.2), kind=kCustom, calls=%fused_computation | custom fusion | bytes 8389632 | tf_op jit(solution)/shard_map/gather | solution.py:22
  223.7 57.9 %all-gather.6.cloned.1.call-done = bf16[1,128,2,128,128]{4,3,2,0,1:T(8,128)(2,1)} async-done(((bf16[1,128,2,32,128]{4,3,2,0,1:T(8,128)(2,1)}), bf16[1,128,2,128,128]{4,3,2,0,1:T(8,128)(2,1)}) %all-gather.6.cloned.1.call-update) | async-done | bytes 8388624 | tf_op jit(solution)/shard_map/all_gather | solution.py:23
  281.6 10.5 %convolution_bitcast_fusion = f32[256,128,64]{1,2,0:T(8,128)S(1)} fusion(bf16[256,128,64]{1,2,0:T(8,128)(2,1)} %gather_fusion, bf16[256,128,128]{2,1,0:T(8,128)(2,1)} %bitcast.78), kind=kOutput, calls=%fused_computation.7 | convolution fusion | flops 536870912 | bytes 20971520 | tf_op jit(solution)/shard_map/tij,tjf->tif/dot_general | solution.py:26
  292.1 7.5 %fusion.5 = bf16[3,128,64]{1,0,2:T(4,128)(2,1)S(1)} fusion(f32[256,128,64]{1,2,0:T(8,128)S(1)} %convolution_bitcast_fusion, f32[3,64,128]{2,1,0:T(8,128)S(1)} %fusion.26, s32[256]{0:T(256)S(1)} %eq.36), kind=kOutput, calls=%fused_computation.9 | convolution fusion | flops 75547392 | bytes 8537088 | tf_op jit(solution)/shard_map/tc,tif->cif/dot_general | solution.py:30
  299.6 1.0 fusion.12
  300.6 29.7 %reduce-scatter.2.cloned.1.call-done = f32[384,64]{0,1:T(8,128)} async-done(((f32[384,256]{0,1:T(8,128)}), f32[384,64]{0,1:T(8,128)}) %reduce-scatter.2.cloned.1.call-update) | async-done | bytes 98320 | tf_op jit(solution)/shard_map/reduce_scatter | solution.py:54
  330.4 1.5 multiply_convert_fusion
  (36 shorter events, 0.8 us)
Async XLA Ops:
  6.5 203.4 %copy-start = (bf16[3,128,128]{2,1,0:T(8,128)(2,1)S(1)}, bf16[3,128,128]{2,1,0:T(8,128)(2,1)}, u32[]{:S(2)}) copy-start(bf16[3,128,128]{2,1,0:T(8,128)(2,1)} %param.14) | copy-start | bytes 294916
  6.5 123.7 %copy-start.3 = (s32[3,128]{1,0:T(4,128)S(1)}, s32[3,128]{1,0:T(4,128)}, u32[]{:S(2)}) copy-start(s32[3,128]{1,0:T(4,128)} %param.13) | copy-start | bytes 4612
  6.5 136.8 %copy-start.5 = (s32[1,128,2]{1,2,0:T(2,128)S(1)}, s32[1,128,2]{1,2,0:T(2,128)}, u32[]{:S(2)}) copy-start(s32[1,128,2]{1,2,0:T(2,128)} %param.10) | copy-start | bytes 3076
  6.5 137.6 %copy-start.1 = (bf16[2048,64]{0,1:T(8,128)(2,1)S(1)}, bf16[2048,64]{0,1:T(8,128)(2,1)}, u32[]{:S(2)}) copy-start(bf16[2048,64]{0,1:T(8,128)(2,1)} %param.12) | copy-start | bytes 786436
  6.5 203.7 %all-gather.4.cloned.1.call-start = ((), (), s32[]{:S(2)}) async-start(), calls=%async_computation.5 | async-start | bytes 6340608 | tf_op jit(solution)/shard_map/all_gather | solution.py:17
  7.3 274.3 %all-gather.6.cloned.1.call-start = ((), (), s32[]{:S(2)}) async-start(), calls=%async_computation.7 | async-start | bytes 10485760 | tf_op jit(solution)/shard_map/all_gather | solution.py:23
  130.2 57.7 %copy-start.4 = (s32[128,1,2]{0,2,1:T(2,128)S(1)}, s32[128,1,2]{0,2,1:T(2,128)}, u32[]{:S(2)}) copy-start(s32[128,1,2]{0,2,1:T(2,128)} %param.11) | copy-start | bytes 3076
  134.8 23.4 %all-to-all-start.2 = ((s32[128,1,9]{2,1,0:T(1,128)}), s32[128,1,9]{2,1,0:T(1,128)S(1)}, u32[]{:S(2)}, u32[]{:S(2)}) async-start(s32[128,1,9]{2,1,0:T(1,128)} %bitcast.9), calls=%async_computation.2 | async-start | bytes 131072 | tf_op jit(solution)/shard_map/all_to_all | solution.py:44
  158.2 22.4 %all-to-all-start = ((bf16[1,128,2]{2,0,1:T(2,128)(2,1)}), bf16[1,128,2]{2,0,1:T(2,128)(2,1)S(1)}, u32[]{:S(2)}, u32[]{:S(2)}) async-start(bf16[1,128,2]{2,0,1:T(2,128)(2,1)} %copy.30), calls=%async_computation | async-start | bytes 131072 | tf_op jit(solution)/shard_map/all_to_all | solution.py:15
  180.6 27.2 %all-to-all-start.3 = ((bf16[128,2,288]{2,1,0:T(2,128)(2,1)}), bf16[128,2,288]{2,1,0:T(2,128)(2,1)S(1)}, u32[]{:S(2)}, u32[]{:S(2)}) async-start(bf16[128,2,288]{2,1,0:T(2,128)(2,1)} %reshape.294), calls=%async_computation.3 | async-start | bytes 393216 | tf_op jit(solution)/shard_map/all_to_all | solution.py:45
  187.9 142.5 %reduce-scatter.2.cloned.1.call-start = ((), (), s32[]{:S(2)}) async-start(), calls=%async_computation.6 | async-start | bytes 491520 | tf_op jit(solution)/shard_map/reduce_scatter | solution.py:54
  292.1 7.5 %copy-start.2 = (bf16[64,256]{1,0:T(8,128)(2,1)S(1)}, bf16[64,256]{1,0:T(8,128)(2,1)}, u32[]{:S(2)}) copy-start(bf16[64,256]{1,0:T(8,128)(2,1)} %param.15) | copy-start | bytes 98308
Sparse Core Ops, SparseCore 0:
  10.4 180.1 all-gather.3
  192.7 88.8 all-gather.5
  300.8 29.5 reduce-scatter.1
where the time goes:
time: 339 us; the launch traced here: 338 us
  waiting for transfers between devices  132 us (39%)
  blocking collectives  123 us (36%)
  local copies, waits for them, and re-layouts  25.4 us (7%)
  starting transfers between devices  23.2 us (7%)
  matrix products  19.2 us (6%)
  between operations  13.4 us (4%)
    all_to_all x1, blocking collectives, per_device(): lax.all_to_all(tiles, 'nodes', split_axis=1, concat_axis=0, tiled=True)  123 us
    all_gather x1, waiting for transfers between devices, per_device(): full_tiles = lax.all_gather(got_tiles, 'feat', axis=3, tiled=True)  57.9 us
    reduce_scatter x1, waiting for transfers between devices, per_device(): lax.psum_scatter(partial_act, 'feat', scatter_dimension=1, tiled=True)  29.7 us
    all_to_all x1, waiting for transfers between devices, per_device(): lax.all_to_all(served, 'nodes', split_axis=0, concat_axis=0, tiled=True)  19.2 us
    all_to_all x1, waiting for transfers between devices, per_device(): lax.all_to_all(requests, 'nodes', split_axis=0, concat_axis=0, tiled=True)  13.8 us
    all_to_all x1, waiting for transfers between devices, per_device(): lax.all_to_all(src_code, 'nodes', split_axis=1, concat_axis=0, tiled=True)  10.7 us
    dot_general x1, matrix products, per_device(): jnp.einsum('tij,tjf->tif', blocks, block_x, preferred_element_type=jnp.fl...  10.5 us
    all_to_all x1, starting transfers between devices, per_device(): lax.all_to_all(requests, 'nodes', split_axis=0, concat_axis=0, tiled=True)  8.54 us
  transfers between devices with their start and end apart: 6, of which 5 were waited for; matrix products, arithmetic and copies ran while one was open for 8% of the time, Pallas kernels for 0%

commit v1 on v0

v1 whole, which is shorter than its diff:
```python
import functools

import jax
import jax.numpy as jnp
from jax import lax
from jax.experimental import pallas as pl
from jax.experimental.pallas import tpu as pltpu
from jax.sharding import PartitionSpec as P

MESH = pl.DeviceIdType.MESH
F32 = jnp.float32
BF16 = jnp.bfloat16
I32 = jnp.int32

X = 4
C = 2
G = X * C
CL = 3
K = 2
CS = 128
SLOTS = 9
PAIR = 16
JP = 5
VR = 48
MARK = 4096


def iota(shape, dim):
    return lax.broadcasted_iota(I32, shape, dim)


def dot_nt(a, b):
    return lax.dot_general(a, b, (((1,), (1,)), ((), ())), preferred_element_type=F32)


def dot_nn(a, b):
    return jnp.dot(a, b, preferred_element_type=F32)


def layer_kernel(
    Z, F, FD, ND,
    x_ref, tiles_ref, src_ref, dst_ref, hist_ref, ids_ref, adj_ref, w_ref, o_ref,
    TV, SV, SSM, XT, XM, WF, ST, ZR, ZR2, AG, ASM, H2, RS, RW, VS, FR, GM, HS, HR,
    LH, OB, PO, PXS, PXR, CHS, CHR, OPS, OPR, OS,
    loc, s_z, r_z, s_g, r_g, s_x, r_x, s_w, r_w, s_t, r_t, s_v, r_v, s_px, r_px, s_c, r_c,
    s_op, r_op, s_rg, r_rg, s_rz, r_rz, s_h, r_h, s_o, r_o,
):
    N = X * Z * C
    FT = F * FD
    RD = CS // F
    RR = CL * RD
    H = Z // 2
    ZB = Z.bit_length() - 1
    NB = ND.bit_length() - 1

    me = lax.axis_index("nodes")
    f = lax.axis_index("feat")
    c = lax.rem(me, C)
    z = lax.rem(me // C, Z)
    x = me // (C * Z)
    oc = 1 - c

    def dev(xx, zz, cc):
        return (xx * Z + zz) * C + cc

    def zp(d):
        return lax.rem(z + d + Z, Z)

    def xp(d):
        return lax.rem(x + d, X)

    def fp(d):
        return lax.rem(f + d, F)

    def rcopy(src, dst, ss, rs, n, ff):
        return pltpu.make_async_remote_copy(
            src_ref=src, dst_ref=dst, send_sem=ss, recv_sem=rs,
            device_id=(n, ff), device_id_type=MESH,
        )

    barrier = pltpu.get_barrier_semaphore()

    def greet(n, ff):
        pl.semaphore_signal(barrier, inc=1, device_id=(n, ff), device_id_type=MESH)

    @pl.loop(1, Z)
    def _(d):
        greet(dev(x, zp(d), c), f)

    for g in range(1, G):
        greet(dev(xp(g // C), z, lax.rem(c + g, C)), f)
    for d in range(1, F):
        greet(me, fp(d))
        greet(dev(x, z, oc), fp(d))

    own_tiles = pltpu.make_async_copy(tiles_ref.at[:, :, c], TV.at[c], loc.at[0])
    own_tiles.start()

    ids = ids_ref[...]
    nid = CL * CS
    row = jnp.concatenate([ids[i : i + 1] for i in range(CL)], axis=1)
    owner = row >> NB
    local = row & (ND - 1)
    o_c = owner & (C - 1)
    o_z = (owner >> 1) & (Z - 1)
    o_x = owner >> (1 + ZB)
    hot = (iota((N, nid), 0) == owner).astype(F32)
    tri = (iota((nid, nid), 0) < iota((nid, nid), 1)).astype(F32).astype(BF16)
    before = dot_nn(hot.astype(BF16), tri)
    rank = jnp.sum(before * hot, axis=0, keepdims=True).astype(I32)
    lane = (o_x * C + o_c) * PAIR + rank
    lane_hot = (iota((G * PAIR, nid), 0) == lane).astype(F32).astype(BF16)
    z_hot = (iota((Z, nid), 0) == o_z).astype(F32)
    hi = (local >> 7).astype(F32)
    lo = (local & 127).astype(F32)
    table = 128.0 * dot_nt((z_hot * hi).astype(BF16), lane_hot) + dot_nt(
        (z_hot * lo).astype(BF16), lane_hot
    )
    asked = dot_nt(z_hot.astype(BF16), lane_hot)
    holder = iota((1, N), 1)
    h_z = (holder >> 1) & (Z - 1)
    h_l = ((holder >> (1 + ZB)) * C + (holder & 1)) * PAIR + SLOTS
    z_hold = (iota((Z, N), 0) == h_z).astype(F32)
    for k in range(K):
        l_hold = (iota((G * PAIR, N), 0) == h_l + k).astype(F32).astype(BF16)
        code = dst_ref[k : k + 1, :].astype(F32)
        table += dot_nt((z_hold * code).astype(BF16), l_hold)
    table = table.astype(I32) + jnp.where(asked > 0.5, 0, MARK)
    for i in range(Z):
        ST[i] = table[i : i + 1]

    pl.semaphore_wait(barrier, Z - 1 + G - 1 + 2 * (F - 1))

    def z_send(d):
        return rcopy(ST.at[zp(d)], ZR.at[z], s_z.at[d], r_z.at[z], dev(x, zp(d), c), f)

    def z_recv(d):
        return rcopy(ST.at[z], ZR.at[zp(d)], s_z.at[d], r_z.at[zp(d)], dev(x, zp(d), c), f)

    @pl.loop(1, Z)
    def _(d):
        z_send(d).start()

    sib = dev(x, z, oc)
    t_send = rcopy(tiles_ref.at[:, :, oc], TV.at[c], s_t.at[0], r_t.at[0], sib, f)
    v_send = rcopy(src_ref, SV.at[c], s_v.at[0], r_v.at[0], sib, f)
    v_send.start()
    t_send.start()

    def x_peer(e):
        return dev(x, z, lax.rem(c + e, C)), lax.rem(c + e, C)

    def x_send(d, e):
        n, _ = x_peer(e)
        return rcopy(
            x_ref, XT.at[c, pl.ds(pl.multiple_of(f * FD, FD), FD)],
            s_x.at[d, e], r_x.at[c, f], n, fp(d),
        )

    def x_recv(d, e):
        n, cc = x_peer(e)
        ff = fp(d)
        return rcopy(
            x_ref, XT.at[cc, pl.ds(pl.multiple_of(ff * FD, FD), FD)],
            s_x.at[d, e], r_x.at[cc, ff], n, ff,
        )

    x_pairs = [(d, e) for e in range(C) for d in range(F) if (d, e) != (0, 0)]
    for d, e in x_pairs:
        x_send(d, e).start()

    def w_send(d):
        return rcopy(w_ref, WF.at[f], s_w.at[d], r_w.at[f], me, fp(d))

    def w_recv(d):
        return rcopy(w_ref, WF.at[fp(d)], s_w.at[d], r_w.at[fp(d)], me, fp(d))

    for d in range(1, F):
        w_send(d).start()

    XT[c, pl.ds(pl.multiple_of(f * FD, FD), FD)] = x_ref[...]
    WF[f] = w_ref[...]
    SV[c] = src_ref[...]
    ZR[z] = ST[z]

    @pl.loop(1, Z)
    def _(d):
        z_recv(d).wait_recv()

    for i in range(Z):
        ZR2[i : i + 1, :] = ZR[i]

    def g_peer(g):
        return xp(g // C), lax.rem(c + g, C)

    def g_send(g):
        gx, gc = g_peer(g)
        return rcopy(ZR2, AG.at[c, x], s_g.at[g], r_g.at[c, x], dev(gx, z, gc), f)

    def g_recv(g):
        gx, gc = g_peer(g)
        return rcopy(ZR2, AG.at[gc, gx], s_g.at[g], r_g.at[gc, gx], dev(gx, z, gc), f)

    for g in range(1, G):
        g_send(g).start()
    AG[c, x] = ZR2[...]

    for d, e in x_pairs:
        x_recv(d, e).wait_recv()
    rcopy(src_ref, SV.at[oc], s_v.at[0], r_v.at[0], sib, f).wait_recv()
    src_copy = pltpu.make_async_copy(SV, SSM, loc.at[1])
    src_copy.start()
    for h in range(C):
        for s in range(CL):
            XM[h, s * CS : (s + 1) * CS, :] = XT[h, :, s * CS : (s + 1) * CS].T
    zero = jnp.zeros((FD, ND), BF16)
    hist = hist_ref[...]
    H2[0, 0:FD] = hist
    H2[0, FD : 2 * FD] = zero
    H2[1, 0:FD] = zero
    H2[1, FD : 2 * FD] = hist

    for g in range(1, G):
        g_recv(g).wait_recv()
    code_copy = pltpu.make_async_copy(AG.at[c], ASM, loc.at[2])
    code_copy.start()
    rcopy(tiles_ref.at[:, :, oc], TV.at[oc], s_t.at[0], r_t.at[0], sib, f).wait_recv()
    own_tiles.wait()
    src_copy.wait()
    code_copy.wait()

    def dirs_of(r):
        return (0,) if r in (0, H) else (0, 1)

    def at(r, d):
        return zp(r) if d == 0 else zp(-r)

    KR = K * RD

    def products(r):
        dirs = dirs_of(r)
        count = len(dirs) * X

        def place(b):
            bx = lax.rem(b, X)
            step = jnp.where(b < X, r, Z - r)
            return lax.rem(x + bx, X), lax.rem(z + step, Z)

        def gather(b, carry):
            tx, tz = place(b)
            n = dev(tx, tz, c)
            for h in range(C):
                for k in range(K):
                    tile = TV[h, tx, tz, k]
                    src = SSM[h, k, n]
                    rows = pl.ds(pl.multiple_of(b * KR + k * RD, RD), RD)
                    for s in range(CL):
                        LH[h, rows, s * CS : (s + 1) * CS] = jnp.where(
                            src == s, tile, jnp.zeros_like(tile)
                        )
            return carry

        lax.fori_loop(0, count, gather, 0)
        m = count * KR
        for h in range(C):
            OB[h, 0:m] = dot_nn(LH[h, 0:m], XM[h])

        def combine(b, carry):
            tx, tz = place(b)
            bx = lax.rem(b, X)
            bd = b // X
            for d in range(CL):
                total = jnp.zeros((RD, FT), F32)
                for h in range(C):
                    for k in range(K):
                        part = OB[h, pl.ds(pl.multiple_of(b * KR + k * RD, RD), RD)]
                        code = ASM[tx, tz, x * (C * PAIR) + h * PAIR + SLOTS + k] - MARK
                        total += jnp.where(code == d, part, jnp.zeros_like(part))
                PO[r, bd, bx, d * RD : (d + 1) * RD] = total
            return carry

        lax.fori_loop(0, count, combine, 0)

    def px(r, d, side):
        to = xp(1 if side == 0 else X - 1)
        return rcopy(
            PXS.at[r, d, side], PXR.at[r, d, side], s_px.at[r, d, side], r_px.at[r, d, side],
            dev(to, z, c), f,
        )

    def send_x(r):
        for d in dirs_of(r):
            for side, bx in ((0, 1), (1, X - 1)):
                PXS[r, d, side] = PO[r, d, bx].astype(BF16)
                px(r, d, side).start()

    def chain(ph, d, r):
        to = zp(1 if d == 0 else -1)
        return rcopy(
            CHS.at[ph, d, r - 1], CHR.at[ph, d, r - 1], s_c.at[ph, d, r - 1],
            r_c.at[ph, d, r - 1], dev(x, to, c), f,
        )

    def live(ph, d, r):
        return r < H or (r == H and d == ph)

    def own(ph, r, d):
        pd = 0 if r in (0, H) else d
        if ph == 0:
            return PO[r, pd, 2]
        return (
            PO[r, pd, 0] + PXR[r, pd, 0].astype(F32) + PXR[r, pd, 1].astype(F32)
        )

    def chain_step(ph, r):
        if ph == 1:
            for d in dirs_of(r):
                for side in range(2):
                    px(r, d, side).wait_recv()
        for d in range(2):
            if not live(ph, d, r):
                continue
            total = own(ph, r, d)
            if live(ph, d, r + 1):
                chain(ph, d, r + 1).wait_recv()
                total = total + CHR[ph, d, r].astype(F32)
            CHS[ph, d, r - 1] = total.astype(BF16)
            chain(ph, d, r).start()

    def chain_end(ph):
        total = own(ph, 0, 0)
        for d in range(2):
            chain(ph, d, 1).wait_recv()
            total = total + CHR[ph, d, 0].astype(F32)
        return total

    def rg_send(g):
        gx, gc = g_peer(g)
        return rcopy(RS.at[gc, gx], RW.at[c, x], s_rg.at[g], r_rg.at[c, x], dev(gx, z, gc), f)

    def rg_recv(g):
        gx, gc = g_peer(g)
        return rcopy(RS.at[c, x], RW.at[gc, gx], s_rg.at[g], r_rg.at[gc, gx], dev(gx, z, gc), f)

    def halo_serve():
        asks = AG[...].reshape(G * Z, G * PAIR).astype(F32)
        lanes = iota((G * Z, G * PAIR), 1)
        base = x * (C * PAIR) + c * PAIR
        KB = min(512, ND)
        for j in range(JP):
            total = jnp.zeros((G * Z, 2 * FD), F32)
            for par in range(2):
                s = 2 * j + par
                if s >= SLOTS:
                    continue
                want = jnp.sum(
                    jnp.where(lanes == base + s, asks, 0.0), axis=1, keepdims=True
                ).astype(I32)
                for b in range(ND // KB):
                    pick = (iota((G * Z, KB), 1) + b * KB == want).astype(F32).astype(BF16)
                    total += dot_nt(pick, H2[par, :, b * KB : (b + 1) * KB])
            RS[:, :, j] = total.astype(BF16).reshape(C, X, Z, 2 * FD)
        for g in range(1, G):
            rg_send(g).start()
        RW[c, x] = RS[c, x]

    def rz_send(d):
        return rcopy(VS.at[zp(d)], FR.at[z], s_rz.at[d], r_rz.at[z], dev(x, zp(d), c), f)

    def rz_recv(d):
        return rcopy(VS.at[z], FR.at[zp(d)], s_rz.at[d], r_rz.at[zp(d)], dev(x, zp(d), c), f)

    def halo_relay():
        for g in range(1, G):
            rg_recv(g).wait_recv()
        rows = RW[...].reshape(G * JP * Z, 2 * FD)
        shape = (VR, G * JP * Z)
        for i in range(Z):
            pick = (iota(shape, 1) == iota(shape, 0) * Z + i).astype(F32).astype(BF16)
            VS[i] = dot_nn(pick, rows).astype(BF16)

        @pl.loop(1, Z)
        def _(d):
            rz_send(d).start()

        FR[z] = VS[z]

    def halo_matrices():
        spot = o_z * VR + (o_c * X + o_x) * JP + (rank >> 1)
        for cl in range(CL):
            cols = slice(cl * CS, (cl + 1) * CS)
            hit = iota((Z * VR, CS), 0) == spot[:, cols]
            odd = rank[:, cols] & 1
            for par in range(2):
                pick = jnp.where(hit, (odd == par).astype(F32), 0.0).astype(BF16)
                GM[par, cols] = dot_nt(adj_ref[cl], pick).astype(BF16)

    def h_send(d):
        return rcopy(HS.at[fp(d)], HR.at[f], s_h.at[d], r_h.at[f], me, fp(d))

    def h_recv(d):
        return rcopy(HS.at[f], HR.at[fp(d)], s_h.at[d], r_h.at[fp(d)], me, fp(d))

    def halo_finish():
        @pl.loop(1, Z)
        def _(d):
            rz_recv(d).wait_recv()

        rows = FR[...].reshape(Z * VR, 2 * FD)
        even = dot_nn(GM[0], rows)
        odd = dot_nn(GM[1], rows)
        halo = even[:, 0:FD] + odd[:, FD : 2 * FD]
        for i in range(F):
            for cl in range(CL):
                at_row = cl * CS + i * RD
                HS[i, cl * RD : (cl + 1) * RD] = halo[at_row : at_row + RD]
        for d in range(1, F):
            h_send(d).start()
        HR[f] = HS[f]

    products(H)
    send_x(H)
    chain_step(0, H)
    products(H - 1)
    send_x(H - 1)
    halo_serve()
    halo_matrices()
    for r in range(H - 1, 0, -1):
        chain_step(0, r)
        chain_step(1, r + 1)
        products(r - 1)
        send_x(r - 1)
        if r == H - 1:
            halo_relay()
    OPS[...] = chain_end(0)
    op = rcopy(OPS, OPR, s_op.at[0], r_op.at[0], dev(xp(2), z, c), f)
    op.start()
    chain_step(1, 1)
    halo_finish()

    for d in range(1, F):
        w_recv(d).wait_recv()
    for d in range(1, F):
        h_recv(d).wait_recv()

    def split(v):
        top = v.astype(BF16)
        return top, (v - top.astype(F32)).astype(BF16)

    act = jnp.zeros((RR, FT), F32)
    for i in range(F):
        top, rest = split(HR[i])
        act += dot_nn(top, WF[i]) + dot_nn(rest, WF[i])
    for side in range(2):
        px(0, 0, side).wait_recv()
    total = chain_end(1)
    op.wait_recv()
    top, rest = split(total + OPR[...])
    weight = WF[...].reshape(FT, FT)
    act += dot_nn(top, weight) + dot_nn(rest, weight)
    out = act / (1.0 + jnp.exp(-act))

    def o_send(d):
        return rcopy(OS.at[fp(d)], o_ref.at[f], s_o.at[d], r_o.at[f], me, fp(d))

    def o_recv(d):
        return rcopy(OS.at[f], o_ref.at[fp(d)], s_o.at[d], r_o.at[fp(d)], me, fp(d))

    for i in range(F):
        OS[i] = out[:, i * FD : (i + 1) * FD].astype(BF16)
    for d in range(1, F):
        o_send(d).start()
    o_ref[f] = OS[f]

    @pl.loop(1, Z)
    def _(d):
        z_send(d).wait_send()
        rz_send(d).wait_send()

    for g in range(1, G):
        g_send(g).wait_send()
        rg_send(g).wait_send()
    t_send.wait_send()
    v_send.wait_send()
    for d, e in x_pairs:
        x_send(d, e).wait_send()
    for d in range(1, F):
        w_send(d).wait_send()
        h_send(d).wait_send()
        o_send(d).wait_send()
    for r in range(H + 1):
        for d in dirs_of(r):
            for side in range(2):
                px(r, d, side).wait_send()
        for ph in range(2):
            for d in range(2):
                if r > 0 and live(ph, d, r):
                    chain(ph, d, r).wait_send()
    op.wait_send()
    for d in range(1, F):
        o_recv(d).wait_recv()


def per_device(F, x_batch, tiles, tile_src, tile_dst, history, halo_ids, halo_adj, weight):
    N = tile_dst.shape[0]
    Z = N // G
    FD = x_batch.shape[1]
    FT = F * FD
    ND = history.shape[0]
    RD = CS // F
    RR = CL * RD
    H = Z // 2
    src_t = tile_src.reshape(N, K).T
    dst_t = tile_dst.reshape(N, K).T
    tiles_v = tiles.reshape(X, Z, C, K, RD, CS)
    vmem = pl.BlockSpec(memory_space=pltpu.VMEM)
    dma = pltpu.SemaphoreType.DMA
    mmax = 2 * X * K * RD
    out = pl.pallas_call(
        functools.partial(layer_kernel, Z, F, FD, ND),
        out_shape=jax.ShapeDtypeStruct((F, RR, FD), BF16),
        in_specs=[vmem, pl.BlockSpec(memory_space=pl.ANY)] + [vmem] * 6,
        out_specs=vmem,
        scratch_shapes=[
            pltpu.VMEM((C, X, Z, K, RD, CS), BF16),
            pltpu.VMEM((C, K, N), I32),
            pltpu.SMEM((C, K, N), I32),
            pltpu.VMEM((C, FT, CL * CS), BF16),
            pltpu.VMEM((C, CL * CS, FT), BF16),
            pltpu.VMEM((F, FD, FT), BF16),
            pltpu.VMEM((Z, 1, G * PAIR), I32),
            pltpu.VMEM((Z, 1, G * PAIR), I32),
            pltpu.VMEM((Z, G * PAIR), I32),
            pltpu.VMEM((C, X, Z, G * PAIR), I32),
            pltpu.SMEM((X, Z, G * PAIR), I32),
            pltpu.VMEM((2, 2 * FD, ND), BF16),
            pltpu.VMEM((C, X, JP, Z, 2 * FD), BF16),
            pltpu.VMEM((C, X, JP, Z, 2 * FD), BF16),
            pltpu.VMEM((Z, VR, 2 * FD), BF16),
            pltpu.VMEM((Z, VR, 2 * FD), BF16),
            pltpu.VMEM((2, CL * CS, Z * VR), BF16),
            pltpu.VMEM((F, RR, FD), F32),
            pltpu.VMEM((F, RR, FD), F32),
            pltpu.VMEM((C, mmax, CL * CS), BF16),
            pltpu.VMEM((C, mmax, FT), F32),
            pltpu.VMEM((H + 1, 2, X, RR, FT), F32),
            pltpu.VMEM((H + 1, 2, 2, RR, FT), BF16),
            pltpu.VMEM((H + 1, 2, 2, RR, FT), BF16),
            pltpu.VMEM((2, 2, H, RR, FT), BF16),
            pltpu.VMEM((2, 2, H, RR, FT), BF16),
            pltpu.VMEM((RR, FT), F32),
            pltpu.VMEM((RR, FT), F32),
            pltpu.VMEM((F, RR, FD), BF16),
            dma((3,)),
            dma((Z,)), dma((Z,)),
            dma((G,)), dma((C, X)),
            dma((F, C)), dma((C, F)),
            dma((F,)), dma((F,)),
            dma((1,)), dma((1,)),
            dma((1,)), dma((1,)),
            dma((H + 1, 2, 2)), dma((H + 1, 2, 2)),
            dma((2, 2, H)), dma((2, 2, H)),
            dma((1,)), dma((1,)),
            dma((G,)), dma((C, X)),
            dma((Z,)), dma((Z,)),
            dma((F,)), dma((F,)),
            dma((F,)), dma((F,)),
        ],
        compiler_params=pltpu.CompilerParams(
            collective_id=0, has_side_effects=True, vmem_limit_bytes=48 * 1024 * 1024
        ),
        name="layer",
    )(x_batch.T, tiles_v, src_t, dst_t, history.T, halo_ids, halo_adj, weight)
    return out.reshape(F, CL, RD, FD).transpose(1, 0, 2, 3).reshape(CL * CS, FD)


def solution(mesh):
    return jax.shard_map(
        functools.partial(per_device, mesh.shape["feat"]),
        mesh=mesh,
        in_specs=(
            P("nodes", "feat"),
            P("nodes", None, None, "feat", None),
            P("nodes", None, None),
            P(None, "nodes", None),
            P("nodes", "feat"),
            P("nodes", None),
            P("nodes", None, None),
            P("feat", None),
        ),
        out_specs=P("nodes", "feat"),
        check_vma=False,
    )
```

time: 339 us -> 87 us (0.26)
  the two profiles are of different devices: /device:TPU:2 before, /device:TPU:16 now
where the time goes in v1:
time: 87 us; the launch traced here: 86.6 us
  Pallas kernels  78.8 us (91%)
  local copies, waits for them, and re-layouts  7.75 us (9%)
    pallas_call x1, Pallas kernels, per_device(): pl.pallas_call(functools.partial(layer_kernel, Z, F, FD, ND), out_shape=j...  78.8 us
    unnamed x16, local copies, waits for them, and re-layouts  7.03 us

profile of v1, /device:TPU:16, one launch (start us, length us, event | category | flops | bytes accessed | tf_op | source)
XLA Modules:
  0.0 86.6 jit_solution(6083925516489071224)
XLA Ops:
  0.0 0.0 copy-start
  0.0 1.6 %copy-done = bf16[1,128,2,32,128]{4,3,2,1,0:T(8,128)(2,1)S(1)} copy-done((bf16[1,128,2,32,128]{4,3,2,1,0:T(8,128)(2,1)S(1)}, bf16[1,128,2,32,128]{4,3,2,1,0:T(8,128)(2,1)}, u32[]{:S(2)}) %copy-start) | copy-done | bytes 2097176
  1.6 0.0 copy-start.1
  1.6 0.9 %copy-done.1 = bf16[2048,64]{0,1:T(8,128)(2,1)S(1)} copy-done((bf16[2048,64]{0,1:T(8,128)(2,1)S(1)}, bf16[2048,64]{0,1:T(8,128)(2,1)}, u32[]{:S(2)}) %copy-start.1) | copy-done | bytes 262168
  2.5 0.0 copy-start.2
  2.5 0.9 %copy-done.2 = bf16[3,128,128]{2,1,0:T(8,128)(2,1)S(1)} copy-done((bf16[3,128,128]{2,1,0:T(8,128)(2,1)S(1)}, bf16[3,128,128]{2,1,0:T(8,128)(2,1)}, u32[]{:S(2)}) %copy-start.2) | copy-done | bytes 98328
  3.4 0.0 copy-start.3
  3.4 0.8 copy-done.3
  4.2 0.0 copy-start.4
  4.2 0.8 copy-done.4
  5.0 0.0 copy-start.5
  5.0 0.7 copy-done.5
  5.7 0.0 copy-start.6
  5.7 0.7 copy-done.6
  6.4 0.0 copy-start.7
  6.4 0.7 copy-done.7
  7.0 78.8 %layer.1 = bf16[4,96,64]{2,1,0:T(8,128)(2,1)S(1)} custom-call(bf16[64,384]{1,0:T(8,128)(2,1)S(1)} %bitcast.16, bf16[4,16,2,2,32,128]{5,4,3,2,1,0:T(8,128)(2,1)S(1)} %bitcast.13, s32[2,128]{1,0:T(2,128)S(1)} %bitcast.17, s32[2,128]{1,0:T(2,128)S(1)} %bitcast.18, bf16[64,2048]{1,0:T(8,128)(2,1)S(1)} %bitcast.15, s32[3,128]{1,0:T(4,128)S(1)} %copy-done.5, ...), custom_call_target="tpu_custom_call" | custom-call | tf_op jit(solution)/shard_map/layer/pallas_call | solution.py:519
  85.9 0.7 copy.11
  (1 shorter events, 0.0 us)
Async XLA Ops:
  0.0 1.6 %copy-start = (bf16[1,128,2,32,128]{4,3,2,1,0:T(8,128)(2,1)S(1)}, bf16[1,128,2,32,128]{4,3,2,1,0:T(8,128)(2,1)}, u32[]{:S(2)}) copy-start(bf16[1,128,2,32,128]{4,3,2,1,0:T(8,128)(2,1)} %param.9) | copy-start | bytes 6291460
  1.6 0.9 %copy-start.1 = (bf16[2048,64]{0,1:T(8,128)(2,1)S(1)}, bf16[2048,64]{0,1:T(8,128)(2,1)}, u32[]{:S(2)}) copy-start(bf16[2048,64]{0,1:T(8,128)(2,1)} %param.12) | copy-start | bytes 786436
  2.5 0.9 %copy-start.2 = (bf16[3,128,128]{2,1,0:T(8,128)(2,1)S(1)}, bf16[3,128,128]{2,1,0:T(8,128)(2,1)}, u32[]{:S(2)}) copy-start(bf16[3,128,128]{2,1,0:T(8,128)(2,1)} %adj_ref.1) | copy-start | bytes 294916
  3.4 0.8 copy-start.3
  4.2 0.8 copy-start.4
  5.0 0.7 copy-start.5
  5.7 0.7 copy-start.6
  6.4 0.7 copy-start.7

commit v2 on v1

v2 whole, which is shorter than its diff:
```python
import functools

import jax
import jax.numpy as jnp
from jax import lax
from jax.experimental import pallas as pl
from jax.experimental.pallas import tpu as pltpu
from jax.sharding import PartitionSpec as P

MESH = pl.DeviceIdType.MESH
F32 = jnp.float32
BF16 = jnp.bfloat16
I32 = jnp.int32

X = 4
C = 2
G = X * C
CL = 3
K = 2
CS = 128
CUT = 0
STEP0 = (1, 1, 1, 1, 1, 1, 1, 1)
STEP1 = (1, 1, 1, 1, 1, 1, 1, 1)
ORDER = [
    "P8", "X8", "A8", "W0", "H0", "H1", "H2", "H3", "H4", "H5", "H6", "H7", "G0",
    "P7", "X7", "A7", "B8", "P6", "X6", "A6", "B7", "R0", "S0",
    "P5", "X5", "A5", "B6", "S1", "P4", "X4", "A4", "B5", "S2", "S3",
    "P3", "X3", "A3", "B4", "S4", "P2", "X2", "A2", "B3", "P1", "X1", "A1", "B2",
    "P0", "X0", "E0", "F0", "B1",
]
SLOTS = 9
PAIR = 16
JP = 5
VR = 48
MARK = 4096


def iota(shape, dim):
    return lax.broadcasted_iota(I32, shape, dim)


def dot_nt(a, b):
    return lax.dot_general(a, b, (((1,), (1,)), ((), ())), preferred_element_type=F32)


def dot_nn(a, b):
    return jnp.dot(a, b, preferred_element_type=F32)


def layer_kernel(
    Z, F, FD, ND, CUT,
    x_hbm, tiles_ref, src_hbm, dst_hbm, hist_hbm, ids_hbm, adj_hbm, w_hbm, o_ref,
    XI, SI, DI, HI, II, AI, WI,
    TV, SV, SSM, XT, XM, WF, ST, ZR, ZR2, AG, ASM, H2, WB, HACC, PK, RS, RW, VS, FR, GM, HS, HR,
    LH, OB, PO, PXS, PXR, CHS, CHR, OPS, OPR, OS,
    loc, s_z, r_z, s_g, r_g, s_x, r_x, s_w, r_w, s_t, r_t, s_v, r_v, s_px, r_px, s_c, r_c,
    s_op, r_op, s_rg, r_rg, s_rz, r_rz, s_h, r_h, s_o, r_o,
):
    N = X * Z * C
    FT = F * FD
    RD = CS // F
    RR = CL * RD
    H = Z // 2
    ZB = Z.bit_length() - 1
    NB = ND.bit_length() - 1

    me = lax.axis_index("nodes")
    f = lax.axis_index("feat")
    c = lax.rem(me, C)
    z = lax.rem(me // C, Z)
    x = me // (C * Z)
    oc = 1 - c
    sib = (x * Z + z) * C + oc

    def dev(xx, zz, cc):
        return (xx * Z + zz) * C + cc

    def zp(d):
        return lax.rem(z + d + Z, Z)

    def xp(d):
        return lax.rem(x + d, X)

    def fp(d):
        return lax.rem(f + d, F)

    def rcopy(src, dst, ss, rs, n, ff):
        return pltpu.make_async_remote_copy(
            src_ref=src, dst_ref=dst, send_sem=ss, recv_sem=rs,
            device_id=(n, ff), device_id_type=MESH,
        )

    begun = {}

    class Exchange:
        def __init__(self, steps, send, recv=None, rolled=False):
            self.steps, self.send, self.recv = steps, send, recv or send
            self.rolled = rolled
            self.received = False

        def each(self, act):
            if self.rolled:
                pl.loop(self.steps[0], self.steps[-1] + 1)(act)
            else:
                for step in self.steps:
                    act(step)

        def begin(self):
            begun[id(self)] = self
            self.each(lambda step: self.send(step).start())

        def arrive(self):
            self.received = True
            self.each(lambda step: self.recv(step).wait_recv())

        def finish(self):
            self.each(lambda step: self.send(step).wait_send())

    def finish_all():
        for e in begun.values():
            if not e.received:
                e.arrive()
            e.finish()

    loads = [
        pltpu.make_async_copy(src, dst, loc.at[i])
        for i, (src, dst) in enumerate(
            [
                (ids_hbm, II), (dst_hbm, DI), (src_hbm, SI), (x_hbm, XI), (w_hbm, WI),
                (hist_hbm, HI), (adj_hbm, AI), (tiles_ref.at[:, :, c], TV.at[c]),
            ]
        )
    ]
    for load in loads:
        load.start()
    l_ids, l_dst, l_src, l_x, l_w, l_hist, l_adj, own_tiles = loads

    barrier = pltpu.get_barrier_semaphore()

    def greet(n, ff):
        pl.semaphore_signal(barrier, inc=1, device_id=(n, ff), device_id_type=MESH)

    @pl.loop(1, Z)
    def _(d):
        greet(dev(x, zp(d), c), f)

    for g in range(1, G):
        greet(dev(xp(g // C), z, lax.rem(c + g, C)), f)
    for d in range(1, F):
        greet(me, fp(d))
        greet(sib, fp(d))

    l_ids.wait()
    l_dst.wait()
    ids = II[...]
    nid = CL * CS
    row = jnp.concatenate([ids[i : i + 1] for i in range(CL)], axis=1)
    owner = row >> NB
    local = row & (ND - 1)
    o_c = owner & (C - 1)
    o_z = (owner >> 1) & (Z - 1)
    o_x = owner >> (1 + ZB)
    hot = (iota((N, nid), 0) == owner).astype(F32)
    tri = (iota((nid, nid), 0) < iota((nid, nid), 1)).astype(F32).astype(BF16)
    before = dot_nn(hot.astype(BF16), tri)
    rank = jnp.sum(before * hot, axis=0, keepdims=True).astype(I32)
    lane = (o_x * C + o_c) * PAIR + rank
    lane_hot = (iota((G * PAIR, nid), 0) == lane).astype(F32).astype(BF16)
    z_hot = (iota((Z, nid), 0) == o_z).astype(F32)
    hi = (local >> 7).astype(F32)
    lo = (local & 127).astype(F32)
    table = 128.0 * dot_nt((z_hot * hi).astype(BF16), lane_hot) + dot_nt(
        (z_hot * lo).astype(BF16), lane_hot
    )
    asked = dot_nt(z_hot.astype(BF16), lane_hot)
    holder = iota((1, N), 1)
    h_z = (holder >> 1) & (Z - 1)
    h_l = ((holder >> (1 + ZB)) * C + (holder & 1)) * PAIR + SLOTS
    z_hold = (iota((Z, N), 0) == h_z).astype(F32)
    for k in range(K):
        l_hold = (iota((G * PAIR, N), 0) == h_l + k).astype(F32).astype(BF16)
        code = DI[k : k + 1, :].astype(F32)
        table += dot_nt((z_hold * code).astype(BF16), l_hold)
    table = table.astype(I32) + jnp.where(asked > 0.5, 0, MARK)
    for i in range(Z):
        ST[i] = table[i : i + 1]

    if CUT == 1:
        for load in loads[2:]:
            load.wait()
    pl.semaphore_wait(barrier, Z - 1 + G - 1 + 2 * (F - 1))
    if CUT == 1:
        o_ref[...] = jnp.zeros_like(o_ref)
        return

    hop_z = Exchange(
        range(1, Z),
        lambda d: rcopy(ST.at[zp(d)], ZR.at[z], s_z.at[d], r_z.at[z], dev(x, zp(d), c), f),
        lambda d: rcopy(ST.at[z], ZR.at[zp(d)], s_z.at[d], r_z.at[zp(d)], dev(x, zp(d), c), f),
        rolled=True,
    )
    hop_z.begin()

    t_swap = Exchange(
        [0],
        lambda _: rcopy(tiles_ref.at[:, :, oc], TV.at[c], s_t.at[0], r_t.at[0], sib, f),
        lambda _: rcopy(tiles_ref.at[:, :, oc], TV.at[oc], s_t.at[0], r_t.at[0], sib, f),
    )
    v_swap = Exchange(
        [0],
        lambda _: rcopy(src_hbm, SV.at[c], s_v.at[0], r_v.at[0], sib, f),
        lambda _: rcopy(src_hbm, SV.at[oc], s_v.at[0], r_v.at[0], sib, f),
    )

    def x_rows(cc, ff):
        return XT.at[cc, pl.ds(pl.multiple_of(ff * FD, FD), FD)]

    def x_core(e):
        return lax.rem(c + e, C)

    x_swap = Exchange(
        [(d, e) for e in range(C) for d in range(F) if (d, e) != (0, 0)],
        lambda p: rcopy(
            x_hbm, x_rows(c, f), s_x.at[p], r_x.at[c, f], dev(x, z, x_core(p[1])), fp(p[0])
        ),
        lambda p: rcopy(
            x_hbm, x_rows(x_core(p[1]), fp(p[0])), s_x.at[p], r_x.at[x_core(p[1]), fp(p[0])],
            dev(x, z, x_core(p[1])), fp(p[0]),
        ),
    )
    w_swap = Exchange(
        range(1, F),
        lambda d: rcopy(w_hbm, WF.at[f], s_w.at[d], r_w.at[f], me, fp(d)),
        lambda d: rcopy(w_hbm, WF.at[fp(d)], s_w.at[d], r_w.at[fp(d)], me, fp(d)),
    )
    v_swap.begin()
    x_swap.begin()
    t_swap.begin()
    w_swap.begin()
    l_src.wait()
    l_x.wait()
    l_w.wait()
    XT[c, pl.ds(pl.multiple_of(f * FD, FD), FD)] = XI[...]
    WF[f] = WI[...]
    SV[c] = SI[...]
    ZR[z] = ST[z]

    l_hist.wait()
    hist = HI[...]
    zero = jnp.zeros((FD, ND), BF16)
    H2[0] = jnp.concatenate([hist, zero], axis=0).T
    H2[1] = jnp.concatenate([zero, hist], axis=0).T
    l_adj.wait()
    spot = o_z * VR + (o_c * X + o_x) * JP + (rank >> 1)
    for cl in range(CL):
        cols = slice(cl * CS, (cl + 1) * CS)
        hit = iota((Z * VR, CS), 0) == spot[:, cols]
        odd = rank[:, cols] & 1
        for par in range(2):
            pick = jnp.where(hit, (odd == par).astype(F32), 0.0).astype(BF16)
            GM[par, cols] = dot_nt(AI[cl], pick).astype(BF16)

    def relay_rows(i, carry):
        shape = (VR, G * JP * Z)
        pick = (iota(shape, 1) == iota(shape, 0) * Z + i).astype(F32).astype(BF16)
        PK[pl.ds(pl.multiple_of(i * VR, VR), VR)] = pick
        return carry

    lax.fori_loop(0, Z, relay_rows, 0)

    hop_z.arrive()
    for i in range(Z):
        ZR2[i : i + 1, :] = ZR[i]

    def g_peer(g):
        return xp(g // C), lax.rem(c + g, C)

    def g_send(g):
        gx, gc = g_peer(g)
        return rcopy(ZR2, AG.at[c, x], s_g.at[g], r_g.at[c, x], dev(gx, z, gc), f)

    def g_recv(g):
        gx, gc = g_peer(g)
        return rcopy(ZR2, AG.at[gc, gx], s_g.at[g], r_g.at[gc, gx], dev(gx, z, gc), f)

    hop_g = Exchange(range(1, G), g_send, g_recv)
    hop_g.begin()
    AG[c, x] = ZR2[...]
    if CUT == 2:
        hop_g.arrive()
        own_tiles.wait()
        finish_all()
        o_ref[...] = jnp.zeros_like(o_ref)
        return

    x_swap.arrive()
    v_swap.arrive()
    src_copy = pltpu.make_async_copy(SV, SSM, loc.at[8])
    src_copy.start()
    for h in range(C):
        for s in range(CL):
            XM[h, s * CS : (s + 1) * CS, :] = XT[h, :, s * CS : (s + 1) * CS].T
    hop_g.arrive()
    code_copy = pltpu.make_async_copy(AG.at[c], ASM, loc.at[9])
    code_copy.start()
    t_swap.arrive()
    own_tiles.wait()
    src_copy.wait()
    code_copy.wait()
    if CUT == 3:
        finish_all()
        o_ref[...] = jnp.zeros_like(o_ref)
        return

    def dirs_of(r):
        return (0,) if r in (0, H) else (0, 1)

    KR = K * RD

    def products(r):
        count = len(dirs_of(r)) * X

        def place(b):
            bx = lax.rem(b, X)
            step = jnp.where(b < X, r, Z - r)
            return lax.rem(x + bx, X), lax.rem(z + step, Z)

        def gather(b, carry):
            tx, tz = place(b)
            n = dev(tx, tz, c)
            for h in range(C):
                for k in range(K):
                    tile = TV[h, tx, tz, k]
                    src = SSM[h, k, n]
                    rows = pl.ds(pl.multiple_of(b * KR + k * RD, RD), RD)
                    for s in range(CL):
                        LH[h, rows, s * CS : (s + 1) * CS] = jnp.where(
                            src == s, tile, jnp.zeros_like(tile)
                        )
            return carry

        lax.fori_loop(0, count, gather, 0)
        m = count * KR
        for h in range(C):
            OB[h, 0:m] = dot_nn(LH[h, 0:m], XM[h])

        def combine(b, carry):
            tx, tz = place(b)
            bx = lax.rem(b, X)
            bd = b // X
            for d in range(CL):
                total = jnp.zeros((RD, FT), F32)
                for h in range(C):
                    for k in range(K):
                        part = OB[h, pl.ds(pl.multiple_of(b * KR + k * RD, RD), RD)]
                        code = ASM[tx, tz, x * (C * PAIR) + h * PAIR + SLOTS + k] - MARK
                        total += jnp.where(code == d, part, jnp.zeros_like(part))
                PO[r, bd, bx, d * RD : (d + 1) * RD] = total
            return carry

        lax.fori_loop(0, count, combine, 0)

    def px_copy(p):
        to = xp(1 if p[2] == 0 else X - 1)
        return rcopy(PXS.at[p], PXR.at[p], s_px.at[p], r_px.at[p], dev(to, z, c), f)

    px = {
        (r, d, side): Exchange([(r, d, side)], px_copy)
        for r in range(H + 1) for d in dirs_of(r) for side in range(2)
    }

    def send_x(r):
        for d in dirs_of(r):
            for side, bx in ((0, 1), (1, X - 1)):
                PXS[r, d, side] = PO[r, d, bx].astype(BF16)
                px[r, d, side].begin()

    def live(ph, d, r):
        return r < H or (r == H and d == ph)

    def step_of(ph, r):
        return (STEP0, STEP1)[ph][r - 1]

    def inputs(ph, d, r):
        return [q for q in range(H, r, -1) if live(ph, d, q) and q - step_of(ph, q) == r]

    def chain_copy(p):
        ph, d, at_r = p
        step = step_of(ph, at_r + 1)
        to = zp(step if d == 0 else -step)
        return rcopy(CHS.at[p], CHR.at[p], s_c.at[p], r_c.at[p], dev(x, to, c), f)

    chain = {
        (ph, d, r): Exchange([(ph, d, r - 1)], chain_copy)
        for ph in range(2) for d in range(2) for r in range(1, H + 1) if live(ph, d, r)
    }

    def own(ph, r, d):
        pd = 0 if r in (0, H) else d
        if ph == 0:
            return PO[r, pd, 2]
        return (
            PO[r, pd, 0] + PXR[r, pd, 0].astype(F32) + PXR[r, pd, 1].astype(F32)
        )

    def chain_step(ph, r):
        if ph == 1:
            for d in dirs_of(r):
                for side in range(2):
                    px[r, d, side].arrive()
        for d in range(2):
            if not live(ph, d, r):
                continue
            total = own(ph, r, d)
            for q in inputs(ph, d, r):
                chain[ph, d, q].arrive()
                total = total + CHR[ph, d, q - 1].astype(F32)
            CHS[ph, d, r - 1] = total.astype(BF16)
            chain[ph, d, r].begin()

    def chain_end(ph):
        total = own(ph, 0, 0)
        for d in range(2):
            for q in inputs(ph, d, 0):
                chain[ph, d, q].arrive()
                total = total + CHR[ph, d, q - 1].astype(F32)
        return total

    def rg_send(g):
        gx, gc = g_peer(g)
        return rcopy(RS.at[gc, gx], RW.at[c, x], s_rg.at[g], r_rg.at[c, x], dev(gx, z, gc), f)

    def rg_recv(g):
        gx, gc = g_peer(g)
        return rcopy(RS.at[c, x], RW.at[gc, gx], s_rg.at[g], r_rg.at[gc, gx], dev(gx, z, gc), f)

    back_g = Exchange(range(1, G), rg_send, rg_recv)

    def halo_wants():
        asks = AG[...].reshape(G * Z, G * PAIR).astype(F32)
        lanes = iota((G * Z, G * PAIR), 1)
        base = x * (C * PAIR) + c * PAIR
        for s in range(SLOTS):
            want = jnp.sum(jnp.where(lanes == base + s, asks, 0.0), axis=1, keepdims=True)
            WB[s] = jnp.broadcast_to(want, (G * Z, CS)).astype(I32)

    KB = min(512, ND)

    def halo_part(par, b):
        slots = range(par, SLOTS, 2)
        wide = iota((G * Z, KB), 1) + b * KB
        pick = jnp.concatenate(
            [
                (wide == jnp.concatenate([WB[s]] * (KB // CS), axis=1)).astype(F32).astype(BF16)
                for s in slots
            ],
            axis=0,
        )
        rows = len(slots) * G * Z
        got = dot_nn(pick, H2[par, b * KB : (b + 1) * KB])
        HACC[0:rows] = got if b == 0 and par == 0 else HACC[0:rows] + got

    def halo_answer():
        for j in range(JP):
            got = HACC[j * G * Z : (j + 1) * G * Z].astype(BF16)
            RS[:, :, j] = got.reshape(C, X, Z, 2 * FD)
        back_g.begin()
        RW[c, x] = RS[c, x]

    back_z = [
        Exchange(
            ds,
            lambda d: rcopy(VS.at[zp(d)], FR.at[z], s_rz.at[d], r_rz.at[z], dev(x, zp(d), c), f),
            lambda d: rcopy(
                VS.at[z], FR.at[zp(d)], s_rz.at[d], r_rz.at[zp(d)], dev(x, zp(d), c), f
            ),
        )
        for ds in [(8, 7, 9), (6, 10, 5), (11, 4, 12), (3, 13, 2), (14, 1, 15)]
    ]

    def halo_relay():
        back_g.arrive()
        rows = RW[...].reshape(G * JP * Z, 2 * FD)
        VS[...] = dot_nn(PK[...], rows).astype(BF16).reshape(Z, VR, 2 * FD)
        FR[z] = VS[z]

    h_swap = Exchange(
        range(1, F),
        lambda d: rcopy(HS.at[fp(d)], HR.at[f], s_h.at[d], r_h.at[f], me, fp(d)),
        lambda d: rcopy(HS.at[f], HR.at[fp(d)], s_h.at[d], r_h.at[fp(d)], me, fp(d)),
    )

    def halo_finish():
        for part in back_z:
            part.arrive()
        rows = FR[...].reshape(Z * VR, 2 * FD)
        even = dot_nn(GM[0], rows)
        odd = dot_nn(GM[1], rows)
        halo = even[:, 0:FD] + odd[:, FD : 2 * FD]
        for i in range(F):
            for cl in range(CL):
                at_row = cl * CS + i * RD
                HS[i, cl * RD : (cl + 1) * RD] = halo[at_row : at_row + RD]
        h_swap.begin()
        HR[f] = HS[f]

    op = Exchange([0], lambda _: rcopy(OPS, OPR, s_op.at[0], r_op.at[0], dev(xp(2), z, c), f))
    parts = [(par, b) for b in range(ND // KB) for par in range(2)]

    def far_sum():
        OPS[...] = chain_end(0).astype(BF16)
        op.begin()

    work = {
        "P": products,
        "X": send_x,
        "A": lambda r: chain_step(0, r),
        "B": lambda r: chain_step(1, r),
        "W": lambda _: halo_wants(),
        "H": lambda i: halo_part(*parts[i]),
        "G": lambda _: halo_answer(),
        "R": lambda _: halo_relay(),
        "S": lambda i: back_z[i].begin(),
        "F": lambda _: halo_finish(),
        "E": lambda _: far_sum(),
    }
    for item in ORDER:
        work[item[0]](int(item[1]))

    w_swap.arrive()
    h_swap.arrive()

    def split(v):
        top = v.astype(BF16)
        return top, (v - top.astype(F32)).astype(BF16)

    act = jnp.zeros((RR, FT), F32)
    for i in range(F):
        top, rest = split(HR[i])
        act += dot_nn(top, WF[i]) + dot_nn(rest, WF[i])
    for side in range(2):
        px[0, 0, side].arrive()
    total = chain_end(1)
    op.arrive()
    top, rest = split(total + OPR[...].astype(F32))
    weight = WF[...].reshape(FT, FT)
    act += dot_nn(top, weight) + dot_nn(rest, weight)
    out = act / (1.0 + jnp.exp(-act))

    o_swap = Exchange(
        range(1, F),
        lambda d: rcopy(OS.at[fp(d)], o_ref.at[f], s_o.at[d], r_o.at[f], me, fp(d)),
        lambda d: rcopy(OS.at[f], o_ref.at[fp(d)], s_o.at[d], r_o.at[fp(d)], me, fp(d)),
    )
    for i in range(F):
        OS[i] = out[:, i * FD : (i + 1) * FD].astype(BF16)
    o_swap.begin()
    o_ref[f] = OS[f]
    finish_all()


def per_device(F, x_batch, tiles, tile_src, tile_dst, history, halo_ids, halo_adj, weight):
    N = tile_dst.shape[0]
    Z = N // G
    FD = x_batch.shape[1]
    FT = F * FD
    ND = history.shape[0]
    RD = CS // F
    RR = CL * RD
    H = Z // 2
    src_t = tile_src.reshape(N, K).T
    dst_t = tile_dst.reshape(N, K).T
    tiles_v = tiles.reshape(X, Z, C, K, RD, CS)
    vmem = pl.BlockSpec(memory_space=pltpu.VMEM)
    hbm = pl.BlockSpec(memory_space=pltpu.HBM)
    dma = pltpu.SemaphoreType.DMA
    mmax = 2 * X * K * RD
    out = pl.pallas_call(
        functools.partial(layer_kernel, Z, F, FD, ND, CUT),
        out_shape=jax.ShapeDtypeStruct((F, RR, FD), BF16),
        in_specs=[hbm] * 8,
        out_specs=vmem,
        scratch_shapes=[
            pltpu.VMEM((FD, CL * CS), BF16),
            pltpu.VMEM((K, N), I32),
            pltpu.VMEM((K, N), I32),
            pltpu.VMEM((FD, ND), BF16),
            pltpu.VMEM((CL, CS), I32),
            pltpu.VMEM((CL, CS, CS), BF16),
            pltpu.VMEM((FD, FT), BF16),
            pltpu.VMEM((C, X, Z, K, RD, CS), BF16),
            pltpu.VMEM((C, K, N), I32),
            pltpu.SMEM((C, K, N), I32),
            pltpu.VMEM((C, FT, CL * CS), BF16),
            pltpu.VMEM((C, CL * CS, FT), BF16),
            pltpu.VMEM((F, FD, FT), BF16),
            pltpu.VMEM((Z, 1, G * PAIR), I32),
            pltpu.VMEM((Z, 1, G * PAIR), I32),
            pltpu.VMEM((Z, G * PAIR), I32),
            pltpu.VMEM((C, X, Z, G * PAIR), I32),
            pltpu.SMEM((X, Z, G * PAIR), I32),
            pltpu.VMEM((2, ND, 2 * FD), BF16),
            pltpu.VMEM((SLOTS, G * Z, CS), I32),
            pltpu.VMEM((JP * G * Z, 2 * FD), F32),
            pltpu.VMEM((Z * VR, G * JP * Z), BF16),
            pltpu.VMEM((C, X, JP, Z, 2 * FD), BF16),
            pltpu.VMEM((C, X, JP, Z, 2 * FD), BF16),
            pltpu.VMEM((Z, VR, 2 * FD), BF16),
            pltpu.VMEM((Z, VR, 2 * FD), BF16),
            pltpu.VMEM((2, CL * CS, Z * VR), BF16),
            pltpu.VMEM((F, RR, FD), F32),
            pltpu.VMEM((F, RR, FD), F32),
            pltpu.VMEM((C, mmax, CL * CS), BF16),
            pltpu.VMEM((C, mmax, FT), F32),
            pltpu.VMEM((H + 1, 2, X, RR, FT), F32),
            pltpu.VMEM((H + 1, 2, 2, RR, FT), BF16),
            pltpu.VMEM((H + 1, 2, 2, RR, FT), BF16),
            pltpu.VMEM((2, 2, H, RR, FT), BF16),
            pltpu.VMEM((2, 2, H, RR, FT), BF16),
            pltpu.VMEM((RR, FT), BF16),
            pltpu.VMEM((RR, FT), BF16),
            pltpu.VMEM((F, RR, FD), BF16),
            dma((10,)),
            dma((Z,)), dma((Z,)),
            dma((G,)), dma((C, X)),
            dma((F, C)), dma((C, F)),
            dma((F,)), dma((F,)),
            dma((1,)), dma((1,)),
            dma((1,)), dma((1,)),
            dma((H + 1, 2, 2)), dma((H + 1, 2, 2)),
            dma((2, 2, H)), dma((2, 2, H)),
            dma((1,)), dma((1,)),
            dma((G,)), dma((C, X)),
            dma((Z,)), dma((Z,)),
            dma((F,)), dma((F,)),
            dma((F,)), dma((F,)),
        ],
        compiler_params=pltpu.CompilerParams(
            collective_id=0, has_side_effects=True, vmem_limit_bytes=60 * 1024 * 1024
        ),
        name="layer",
    )(x_batch.T, tiles_v, src_t, dst_t, history.T, halo_ids, halo_adj, weight)
    return out.reshape(F, CL, RD, FD).transpose(1, 0, 2, 3).reshape(CL * CS, FD)


def solution(mesh):
    return jax.shard_map(
        functools.partial(per_device, mesh.shape["feat"]),
        mesh=mesh,
        in_specs=(
            P("nodes", "feat"),
            P("nodes", None, None, "feat", None),
            P("nodes", None, None),
            P(None, "nodes", None),
            P("nodes", "feat"),
            P("nodes", None),
            P("nodes", None, None),
            P("feat", None),
        ),
        out_specs=P("nodes", "feat"),
        check_vma=False,
    )
```

time: 87 us -> 76.2 us (0.88)
  the two profiles are of different devices: /device:TPU:16 before, /device:TPU:2 now
where the time goes in v2:
time: 76.2 us; the launch traced here: 76.1 us
  Pallas kernels  74.4 us (98%)
  local copies, waits for them, and re-layouts  1.61 us (2%)
    pallas_call x1, Pallas kernels, per_device(): pl.pallas_call(functools.partial(layer_kernel, Z, F, FD, ND, CUT), out_sh...  74.4 us
    reshape x2, local copies, waits for them, and re-layouts, per_device(): return out.reshape(F, CL, RD, FD).transpose(1, 0, 2, 3).reshape(CL * CS, FD)  1.61 us

profile of v2, /device:TPU:2, one launch (start us, length us, event | category | flops | bytes accessed | tf_op | source)
XLA Modules:
  0.0 76.1 jit_solution(3743536919952189417)
XLA Ops:
  0.0 74.4 %layer.1 = bf16[4,96,64]{2,1,0:T(8,128)(2,1)} custom-call(bf16[64,384]{1,0:T(8,128)(2,1)} %bitcast.17, bf16[4,16,2,2,32,128]{5,4,3,2,1,0:T(8,128)(2,1)} %bitcast.13, s32[2,128]{1,0:T(2,128)} %bitcast.18, s32[2,128]{1,0:T(2,128)} %bitcast.19, bf16[64,2048]{1,0:T(8,128)(2,1)} %bitcast.16, s32[3,128]{1,0:T(4,128)} %ids_hbm.1, bf16[3,128,128]{2,1,0:T(8,128)(2,1)} %adj_hbm.1, ...), custom_call_target="tpu_custom_call" | custom-call | tf_op jit(solution)/shard_map/layer/pallas_call | solution.py:578
  74.4 0.9 %copy.10 = bf16[4,3,32,64]{3,2,0,1:T(8,128)(2,1)S(1)} copy(bf16[4,3,32,64]{3,2,1,0:T(8,128)(2,1)} %bitcast.14) | data formatting | bytes 98304 | tf_op jit(solution)/shard_map/reshape | solution.py:643
  75.4 0.7 copy.11

commit v3 on v2

--- a/solution.py
+++ b/solution.py
@@ -18,15 +18,12 @@
 CL = 3
 K = 2
 CS = 128
-CUT = 0
-STEP0 = (1, 1, 1, 1, 1, 1, 1, 1)
-STEP1 = (1, 1, 1, 1, 1, 1, 1, 1)
+STEP = (1, 2, 1, 2, 1, 2, 1, 2)
 ORDER = [
-    "P8", "X8", "A8", "W0", "H0", "H1", "H2", "H3", "H4", "H5", "H6", "H7", "G0",
-    "P7", "X7", "A7", "B8", "P6", "X6", "A6", "B7", "R0", "S0",
-    "P5", "X5", "A5", "B6", "S1", "P4", "X4", "A4", "B5", "S2", "S3",
-    "P3", "X3", "A3", "B4", "S4", "P2", "X2", "A2", "B3", "P1", "X1", "A1", "B2",
-    "P0", "X0", "E0", "F0", "B1",
+    "P8", "X8", "P7", "X7", "P6", "X6", "W0", "H0", "H1", "H2", "H3", "H4", "H5", "H6", "H7",
+    "G0", "Y8", "Y7", "P5", "X5", "Y6", "P4", "X4", "B8", "B7", "R0", "S0", "Y5", "P3", "X3",
+    "B6", "S1", "Y4", "P2", "X2", "S2", "B5", "Y3", "P1", "X1", "B4", "S3", "Y2", "P0", "X0",
+    "B3", "S4", "Y1", "Y0", "B2", "F0", "B1",
 ]
 SLOTS = 9
 PAIR = 16
@@ -48,13 +45,13 @@
 
 
 def layer_kernel(
-    Z, F, FD, ND, CUT,
+    Z, F, FD, ND,
     x_hbm, tiles_ref, src_hbm, dst_hbm, hist_hbm, ids_hbm, adj_hbm, w_hbm, o_ref,
     XI, SI, DI, HI, II, AI, WI,
     TV, SV, SSM, XT, XM, WF, ST, ZR, ZR2, AG, ASM, H2, WB, HACC, PK, RS, RW, VS, FR, GM, HS, HR,
-    LH, OB, PO, PXS, PXR, CHS, CHR, OPS, OPR, OS,
-    loc, s_z, r_z, s_g, r_g, s_x, r_x, s_w, r_w, s_t, r_t, s_v, r_v, s_px, r_px, s_c, r_c,
-    s_op, r_op, s_rg, r_rg, s_rz, r_rz, s_h, r_h, s_o, r_o,
+    LH, OB, PO, OXS, OXR, PXS, PXR, CHS, CHR, OS,
+    loc, s_z, r_z, s_g, r_g, s_x, r_x, s_w, r_w, s_t, r_t, s_v, r_v, s_ox, r_ox, s_px, r_px, s_c, r_c,
+    s_rg, r_rg, s_rz, r_rz, s_h, r_h, s_o, r_o,
 ):
     N = X * Z * C
     FT = F * FD
@@ -185,13 +182,7 @@
     for i in range(Z):
         ST[i] = table[i : i + 1]
 
-    if CUT == 1:
-        for load in loads[2:]:
-            load.wait()
     pl.semaphore_wait(barrier, Z - 1 + G - 1 + 2 * (F - 1))
-    if CUT == 1:
-        o_ref[...] = jnp.zeros_like(o_ref)
-        return
 
     hop_z = Exchange(
         range(1, Z),
@@ -286,12 +277,6 @@
     hop_g = Exchange(range(1, G), g_send, g_recv)
     hop_g.begin()
     AG[c, x] = ZR2[...]
-    if CUT == 2:
-        hop_g.arrive()
-        own_tiles.wait()
-        finish_all()
-        o_ref[...] = jnp.zeros_like(o_ref)
-        return
 
     x_swap.arrive()
     v_swap.arrive()
@@ -307,10 +292,6 @@
     own_tiles.wait()
     src_copy.wait()
     code_copy.wait()
-    if CUT == 3:
-        finish_all()
-        o_ref[...] = jnp.zeros_like(o_ref)
-        return
 
     def dirs_of(r):
         return (0,) if r in (0, H) else (0, 1)
@@ -360,70 +341,82 @@
 
         lax.fori_loop(0, count, combine, 0)
 
+    HF = RR // 2
+    halves = (slice(0, HF), slice(HF, RR))
+    sides = (1, X - 1)
+
+    def half_of(h):
+        return pl.ds(h * HF, HF)
+
+    def ox_copy(p):
+        to = xp(sides[p[2]])
+        return rcopy(OXS.at[p], OXR.at[p], s_ox.at[p], r_ox.at[p], dev(to, z, c), f)
+
     def px_copy(p):
-        to = xp(1 if p[2] == 0 else X - 1)
-        return rcopy(PXS.at[p], PXR.at[p], s_px.at[p], r_px.at[p], dev(to, z, c), f)
-
-    px = {
-        (r, d, side): Exchange([(r, d, side)], px_copy)
-        for r in range(H + 1) for d in dirs_of(r) for side in range(2)
-    }
+        to = xp(sides[p[2]])
+        at_p = (p[0], p[1], p[2], half_of(p[3]))
+        return rcopy(PXS.at[at_p], PXR.at[at_p], s_px.at[p], r_px.at[p], dev(to, z, c), f)
+
+    ways = [(r, d, side) for r in range(H + 1) for d in dirs_of(r) for side in range(2)]
+    ox = {p: Exchange([p], ox_copy) for p in ways}
+    px = {(*p, h): Exchange([(*p, h)], px_copy) for p in ways for h in range(2)}
 
     def send_x(r):
         for d in dirs_of(r):
-            for side, bx in ((0, 1), (1, X - 1)):
-                PXS[r, d, side] = PO[r, d, bx].astype(BF16)
-                px[r, d, side].begin()
-
-    def live(ph, d, r):
-        return r < H or (r == H and d == ph)
-
-    def step_of(ph, r):
-        return (STEP0, STEP1)[ph][r - 1]
-
-    def inputs(ph, d, r):
-        return [q for q in range(H, r, -1) if live(ph, d, q) and q - step_of(ph, q) == r]
+            for side, bx in enumerate(sides):
+                OXS[r, d, side] = PO[r, d, 2, halves[side]].astype(BF16)
+                ox[r, d, side].begin()
+            for side, bx in enumerate(sides):
+                rows = halves[1 - side]
+                PXS[r, d, side, rows] = PO[r, d, bx, rows].astype(BF16)
+                px[r, d, side, 1 - side].begin()
+
+    def send_y(r):
+        for d in dirs_of(r):
+            for side, bx in enumerate(sides):
+                ox[r, d, side].arrive()
+                rows = halves[side]
+                total = PO[r, d, bx, rows] + OXR[r, d, side].astype(F32)
+                PXS[r, d, side, rows] = total.astype(BF16)
+                px[r, d, side, side].begin()
+
+    def live(d, r):
+        return r < H or (r == H and d == 0)
+
+    def inputs(d, r):
+        return [q for q in range(H, r, -1) if live(d, q) and q - STEP[q - 1] == r]
 
     def chain_copy(p):
-        ph, d, at_r = p
-        step = step_of(ph, at_r + 1)
-        to = zp(step if d == 0 else -step)
+        d, at_r = p
+        to = zp(STEP[at_r] if d == 0 else -STEP[at_r])
         return rcopy(CHS.at[p], CHR.at[p], s_c.at[p], r_c.at[p], dev(x, to, c), f)
 
     chain = {
-        (ph, d, r): Exchange([(ph, d, r - 1)], chain_copy)
-        for ph in range(2) for d in range(2) for r in range(1, H + 1) if live(ph, d, r)
+        (d, r): Exchange([(d, r - 1)], chain_copy)
+        for d in range(2) for r in range(1, H + 1) if live(d, r)
     }
 
-    def own(ph, r, d):
-        pd = 0 if r in (0, H) else d
-        if ph == 0:
-            return PO[r, pd, 2]
-        return (
-            PO[r, pd, 0] + PXR[r, pd, 0].astype(F32) + PXR[r, pd, 1].astype(F32)
-        )
-
-    def chain_step(ph, r):
-        if ph == 1:
-            for d in dirs_of(r):
-                for side in range(2):
-                    px[r, d, side].arrive()
+    def own(r, d):
+        for side in range(2):
+            for h in range(2):
+                px[r, d, side, h].arrive()
+        return PO[r, d, 0] + PXR[r, d, 0].astype(F32) + PXR[r, d, 1].astype(F32)
+
+    def chain_step(r):
+        for d in dirs_of(r):
+            total = own(r, d)
+            for q in inputs(d, r):
+                chain[d, q].arrive()
+                total = total + CHR[d, q - 1].astype(F32)
+            CHS[d, r - 1] = total.astype(BF16)
+            chain[d, r].begin()
+
+    def chain_end():
+        total = own(0, 0)
         for d in range(2):
-            if not live(ph, d, r):
-                continue
-            total = own(ph, r, d)
-            for q in inputs(ph, d, r):
-                chain[ph, d, q].arrive()
-                total = total + CHR[ph, d, q - 1].astype(F32)
-            CHS[ph, d, r - 1] = total.astype(BF16)
-            chain[ph, d, r].begin()
-
-    def chain_end(ph):
-        total = own(ph, 0, 0)
-        for d in range(2):
-            for q in inputs(ph, d, 0):
-                chain[ph, d, q].arrive()
-                total = total + CHR[ph, d, q - 1].astype(F32)
+            for q in inputs(d, 0):
+                chain[d, q].arrive()
+                total = total + CHR[d, q - 1].astype(F32)
         return total
 
     def rg_send(g):
@@ -504,25 +497,19 @@
         h_swap.begin()
         HR[f] = HS[f]
 
-    op = Exchange([0], lambda _: rcopy(OPS, OPR, s_op.at[0], r_op.at[0], dev(xp(2), z, c), f))
     parts = [(par, b) for b in range(ND // KB) for par in range(2)]
-
-    def far_sum():
-        OPS[...] = chain_end(0).astype(BF16)
-        op.begin()
 
     work = {
         "P": products,
         "X": send_x,
-        "A": lambda r: chain_step(0, r),
-        "B": lambda r: chain_step(1, r),
+        "Y": send_y,
+        "B": chain_step,
         "W": lambda _: halo_wants(),
         "H": lambda i: halo_part(*parts[i]),
         "G": lambda _: halo_answer(),
         "R": lambda _: halo_relay(),
         "S": lambda i: back_z[i].begin(),
         "F": lambda _: halo_finish(),
-        "E": lambda _: far_sum(),
     }
     for item in ORDER:
         work[item[0]](int(item[1]))
@@ -538,11 +525,7 @@
     for i in range(F):
         top, rest = split(HR[i])
         act += dot_nn(top, WF[i]) + dot_nn(rest, WF[i])
-    for side in range(2):
-        px[0, 0, side].arrive()
-    total = chain_end(1)
-    op.arrive()
-    top, rest = split(total + OPR[...].astype(F32))
+    top, rest = split(chain_end())
     weight = WF[...].reshape(FT, FT)
     act += dot_nn(top, weight) + dot_nn(rest, weight)
     out = act / (1.0 + jnp.exp(-act))
@@ -576,7 +559,7 @@
     dma = pltpu.SemaphoreType.DMA
     mmax = 2 * X * K * RD
     out = pl.pallas_call(
-        functools.partial(layer_kernel, Z, F, FD, ND, CUT),
+        functools.partial(layer_kernel, Z, F, FD, ND),
         out_shape=jax.ShapeDtypeStruct((F, RR, FD), BF16),
         in_specs=[hbm] * 8,
         out_specs=vmem,
@@ -613,12 +596,12 @@
             pltpu.VMEM((C, mmax, CL * CS), BF16),
             pltpu.VMEM((C, mmax, FT), F32),
             pltpu.VMEM((H + 1, 2, X, RR, FT), F32),
+            pltpu.VMEM((H + 1, 2, 2, RR // 2, FT), BF16),
+            pltpu.VMEM((H + 1, 2, 2, RR // 2, FT), BF16),
             pltpu.VMEM((H + 1, 2, 2, RR, FT), BF16),
             pltpu.VMEM((H + 1, 2, 2, RR, FT), BF16),
-            pltpu.VMEM((2, 2, H, RR, FT), BF16),
-            pltpu.VMEM((2, 2, H, RR, FT), BF16),
-            pltpu.VMEM((RR, FT), BF16),
-            pltpu.VMEM((RR, FT), BF16),
+            pltpu.VMEM((2, H, RR, FT), BF16),
+            pltpu.VMEM((2, H, RR, FT), BF16),
             pltpu.VMEM((F, RR, FD), BF16),
             dma((10,)),
             dma((Z,)), dma((Z,)),
@@ -628,8 +611,8 @@
             dma((1,)), dma((1,)),
             dma((1,)), dma((1,)),
             dma((H + 1, 2, 2)), dma((H + 1, 2, 2)),
-            dma((2, 2, H)), dma((2, 2, H)),
-            dma((1,)), dma((1,)),
+            dma((H + 1, 2, 2, 2)), dma((H + 1, 2, 2, 2)),
+            dma((2, H)), dma((2, H)),
             dma((G,)), dma((C, X)),
             dma((Z,)), dma((Z,)),
             dma((F,)), dma((F,)),

time: 76.2 us -> 74.2 us (0.974)
  Pallas kernels: 74.4 us -> 72.4 us
    pallas_call x1, Pallas kernels: 74.4 us -> 72.4 us  [per_device(): pl.pallas_call(functools.partial(layer_kernel, Z, F, FD, ND), out_shape=j...]
where the time goes in v3:
time: 74.2 us; the launch traced here: 74 us
  Pallas kernels  72.4 us (98%)
  local copies, waits for them, and re-layouts  1.61 us (2%)
    pallas_call x1, Pallas kernels, per_device(): pl.pallas_call(functools.partial(layer_kernel, Z, F, FD, ND), out_shape=j...  72.4 us
    reshape x2, local copies, waits for them, and re-layouts, per_device(): return out.reshape(F, CL, RD, FD).transpose(1, 0, 2, 3).reshape(CL * CS, FD)  1.61 us

profile of v3, /device:TPU:2, one launch (start us, length us, event | category | flops | bytes accessed | tf_op | source)
XLA Modules:
  0.0 74.0 jit_solution(15299799372242004317)
XLA Ops:
  0.0 72.4 %layer.1 = bf16[4,96,64]{2,1,0:T(8,128)(2,1)} custom-call(bf16[64,384]{1,0:T(8,128)(2,1)} %bitcast.17, bf16[4,16,2,2,32,128]{5,4,3,2,1,0:T(8,128)(2,1)} %bitcast.13, s32[2,128]{1,0:T(2,128)} %bitcast.18, s32[2,128]{1,0:T(2,128)} %bitcast.19, bf16[64,2048]{1,0:T(8,128)(2,1)} %bitcast.16, s32[3,128]{1,0:T(4,128)} %ids_hbm.1, bf16[3,128,128]{2,1,0:T(8,128)(2,1)} %adj_hbm.1, ...), custom_call_target="tpu_custom_call" | custom-call | tf_op jit(solution)/shard_map/layer/pallas_call | solution.py:561
  72.4 0.9 %copy.10 = bf16[4,3,32,64]{3,2,0,1:T(8,128)(2,1)S(1)} copy(bf16[4,3,32,64]{3,2,1,0:T(8,128)(2,1)} %bitcast.14) | data formatting | bytes 98304 | tf_op jit(solution)/shard_map/reshape | solution.py:626
  73.3 0.7 copy.11

commit v4 on v3

--- a/solution.py
+++ b/solution.py
@@ -68,6 +68,7 @@
     x = me // (C * Z)
     oc = 1 - c
     sib = (x * Z + z) * C + oc
+    FAR = sorted(range(1, Z), key=lambda d: -min(d, Z - d))
 
     def dev(xx, zz, cc):
         return (xx * Z + zz) * C + cc
@@ -137,8 +138,7 @@
     def greet(n, ff):
         pl.semaphore_signal(barrier, inc=1, device_id=(n, ff), device_id_type=MESH)
 
-    @pl.loop(1, Z)
-    def _(d):
+    for d in FAR:
         greet(dev(x, zp(d), c), f)
 
     for g in range(1, G):
@@ -185,10 +185,9 @@
     pl.semaphore_wait(barrier, Z - 1 + G - 1 + 2 * (F - 1))
 
     hop_z = Exchange(
-        range(1, Z),
+        FAR,
         lambda d: rcopy(ST.at[zp(d)], ZR.at[z], s_z.at[d], r_z.at[z], dev(x, zp(d), c), f),
         lambda d: rcopy(ST.at[z], ZR.at[zp(d)], s_z.at[d], r_z.at[zp(d)], dev(x, zp(d), c), f),
-        rolled=True,
     )
     hop_z.begin()
 

time: 74.2 us -> 74.1 us (level)
  no operation moved by 1% of the time
where the time goes in v4:
time: 74.1 us; the launch traced here: 73.9 us
  Pallas kernels  72.3 us (98%)
  local copies, waits for them, and re-layouts  1.61 us (2%)
    pallas_call x1, Pallas kernels, per_device(): pl.pallas_call(functools.partial(layer_kernel, Z, F, FD, ND), out_shape=j...  72.3 us
    reshape x2, local copies, waits for them, and re-layouts, per_device(): return out.reshape(F, CL, RD, FD).transpose(1, 0, 2, 3).reshape(CL * CS, FD)  1.61 us

profile of v4, /device:TPU:2, one launch (start us, length us, event | category | flops | bytes accessed | tf_op | source)
XLA Modules:
  0.0 73.9 jit_solution(14084898629749464438)
XLA Ops:
  0.0 72.3 %layer.1 = bf16[4,96,64]{2,1,0:T(8,128)(2,1)} custom-call(bf16[64,384]{1,0:T(8,128)(2,1)} %bitcast.17, bf16[4,16,2,2,32,128]{5,4,3,2,1,0:T(8,128)(2,1)} %bitcast.13, s32[2,128]{1,0:T(2,128)} %bitcast.18, s32[2,128]{1,0:T(2,128)} %bitcast.19, bf16[64,2048]{1,0:T(8,128)(2,1)} %bitcast.16, s32[3,128]{1,0:T(4,128)} %ids_hbm.1, bf16[3,128,128]{2,1,0:T(8,128)(2,1)} %adj_hbm.1, ...), custom_call_target="tpu_custom_call" | custom-call | tf_op jit(solution)/shard_map/layer/pallas_call | solution.py:560
  72.3 0.9 %copy.10 = bf16[4,3,32,64]{3,2,0,1:T(8,128)(2,1)S(1)} copy(bf16[4,3,32,64]{3,2,1,0:T(8,128)(2,1)} %bitcast.14) | data formatting | bytes 98304 | tf_op jit(solution)/shard_map/reshape | solution.py:625
  73.2 0.7 copy.11
